TPU v7x, 32 devices: a whole 2x2x4 slice. The times are simulated.
32 devices in a mesh: frow: 8 (over z, y), fcol: 4 (over x, core).
Axes of the slice: x: 2, y: 2, z: 4, core: 2. Of those that a mesh axis runs over, the one named last changes fastest.
Arguments:
- front_orig: float32 [8, 2048, 4, 4096], P('frow', None, 'fcol'), may hold values from -0.1 to 45, as said below
- child_tiles: bfloat16 [2048, 128, 128], P(('frow', 'fcol')), may hold values from -0.25 to 0.25
- tile_target: int32 [2048, 2], P(('frow', 'fcol')), may hold values from 0 to 511, as said below
- tile_rows: int32 [2048, 128], P(('frow', 'fcol')), may hold values from 0 to 127, each once within a row
- tile_cols: int32 [2048, 128], P(('frow', 'fcol')), may hold values from 0 to 127, each once within a row
Outputs:
- front_out: float32 [8, 2048, 4, 4096], P('frow', None, 'fcol')
Inputs may be any that keep to these rules, and one draw needn't show every extreme that they name: `front_orig`: Symmetric; the lower triangle of the front after every tile is added defines a positive definite matrix. `tile_target`: rows come 64 to a device in device order. Column 0 is the owner, frow index times 4 plus fcol index; column 1 the local block on that owner, local block row times 32 plus local block column; the block lies on or below the front's block diagonal. At most 2 tiles of one device go to one owner, and one owner receives exactly 2 from every device.
All inputs are finite; a program needn't handle non-finite values.
Results may differ from a plain program's by a relative error of at most 0.0003.
Values may be sent and summed in bfloat16 or wider, within the bound.
A program may use at most 192 MiB of HBM per device.

v0:
```python
import jax
import jax.numpy as jnp
from jax import lax
from jax.sharding import PartitionSpec as P

PW = 512
NPANEL = 2
CAP = 2


def as_sent(x):
    return jax.tree.map(lambda a: a.astype(jnp.bfloat16) if a.dtype == jnp.float32 else a, x)


def broadcast(block, axis, source):
    block = jnp.where(lax.axis_index(axis) == source, block, jnp.zeros_like(block))
    return lax.psum(block, axis)


def place_tiles(received):
    tile_block, perm_block, target_block = received
    width = tile_block.shape[-1]
    positions = jnp.arange(width, dtype=jnp.int32)
    row_onehot = (perm_block[:, :, 0, None, :] == positions[:, None]).astype(jnp.bfloat16)
    col_onehot = (perm_block[:, :, 1, None, :] == positions[:, None]).astype(jnp.bfloat16)
    moved = jnp.einsum(
        "abxi,abij->abxj", row_onehot, tile_block, preferred_element_type=jnp.float32
    ).astype(jnp.bfloat16)
    placed = jnp.einsum(
        "abxj,abyj->abxy", moved, col_onehot, preferred_element_type=jnp.float32
    ).astype(jnp.bfloat16)
    return (placed, target_block)


def subtract_product(matrix, row_factor, col_factor):
    product = jnp.dot(
        row_factor,
        col_factor.T,
        precision=lax.Precision.HIGHEST,
        preferred_element_type=jnp.float32,
    )
    return matrix - product


def shards(front_orig, child_tiles, tile_target, tile_rows, tile_cols):
    row_devs = lax.axis_size("frow")
    col_devs = lax.axis_size("fcol")
    owners = row_devs * col_devs
    row_here = lax.axis_index("frow")
    col_here = lax.axis_index("fcol")
    width = child_tiles.shape[1]
    held = child_tiles.shape[0]
    slot_count = owners * CAP
    owner_of = tile_target[:, 0]
    block_of = tile_target[:, 1]
    tile_order = jnp.arange(held, dtype=jnp.int32)
    same_owner = owner_of[:, None] == owner_of[None, :]
    earlier = tile_order[None, :] < tile_order[:, None]
    rank_of = jnp.sum(jnp.where(same_owner & earlier, 1, 0), axis=1).astype(jnp.int32)
    slot_of = owner_of * CAP + rank_of
    slot_match = slot_of[None, :] == jnp.arange(slot_count, dtype=jnp.int32)[:, None]
    source_tile = jnp.sum(jnp.where(slot_match, tile_order[None, :], 0), axis=1)
    filled = jnp.any(slot_match, axis=1)
    send_tiles = jnp.where(
        filled[:, None, None],
        jnp.take(child_tiles, source_tile, axis=0),
        jnp.zeros((), jnp.bfloat16),
    )
    send_perms = jnp.stack(
        [jnp.take(tile_rows, source_tile, axis=0), jnp.take(tile_cols, source_tile, axis=0)], axis=1
    )
    send_blocks = jnp.take(block_of, source_tile, axis=0)
    placed, blocks_in = place_tiles(
        (
            lax.all_to_all(
                send_tiles.reshape(owners, CAP, width, width),
                ("frow", "fcol"),
                split_axis=0,
                concat_axis=0,
                tiled=True,
            ),
            lax.all_to_all(
                send_perms.reshape(owners, CAP, 2, width),
                ("frow", "fcol"),
                split_axis=0,
                concat_axis=0,
                tiled=True,
            ),
            lax.all_to_all(
                send_blocks.reshape(owners, CAP),
                ("frow", "fcol"),
                split_axis=0,
                concat_axis=0,
                tiled=True,
            ),
        )
    )
    local = front_orig[0, :, 0, :]
    row_blocks = local.shape[0] // width
    col_blocks = local.shape[1] // width
    block_ids = jnp.arange(row_blocks * col_blocks, dtype=jnp.int32)
    block_onehot = (blocks_in.reshape(1, slot_count) == block_ids[:, None]).astype(jnp.bfloat16)
    summed = jnp.dot(
        block_onehot, placed.reshape(slot_count, width * width), preferred_element_type=jnp.float32
    )
    added = (
        summed.reshape(row_blocks, col_blocks, width, width)
        .transpose(0, 2, 1, 3)
        .reshape(local.shape)
    )
    matrix = local + added
    local_rows = jnp.arange(local.shape[0], dtype=jnp.int32)
    local_cols = jnp.arange(local.shape[1], dtype=jnp.int32)
    global_rows = (local_rows // width * row_devs + row_here) * width + local_rows % width
    global_cols = (local_cols // width * col_devs + col_here) * width + local_cols % width
    panel_blocks = PW // width
    ratio = row_devs // col_devs
    for panel_idx in range(NPANEL):
        start = panel_idx * PW
        stop = start + PW
        first_block = panel_idx * panel_blocks
        col_slot = first_block // col_devs
        col_first = first_block % col_devs
        row_slot = first_block // row_devs
        row_first = first_block % row_devs
        own_column = matrix[:, col_slot * width : (col_slot + 1) * width]
        wide_panel = lax.all_gather(
            own_column.astype(jnp.bfloat16), "fcol", axis=1, tiled=True
        ).astype(own_column.dtype)
        panel = wide_panel[:, col_first * width : col_first * width + PW]
        diag_rows = lax.all_gather(
            panel[row_slot * width : (row_slot + 1) * width].astype(jnp.bfloat16),
            "frow",
            axis=0,
            tiled=True,
        ).astype(jnp.float32)
        diag_block = diag_rows[row_first * width : row_first * width + PW]
        symmetric = jnp.tril(diag_block) + jnp.tril(diag_block, -1).T
        factor = jnp.linalg.cholesky(symmetric)
        solved = lax.linalg.triangular_solve(
            factor, panel, left_side=False, lower=True, transpose_a=True
        )
        below = (global_rows >= stop)[:, None]
        inside = (global_rows >= start)[:, None]
        factor_rows = jnp.take(factor, jnp.clip(global_rows - start, 0, PW - 1), axis=0)
        new_panel = jnp.where(below, solved, jnp.where(inside, factor_rows, 0.0))
        row_factor = jnp.where(below, solved, 0.0)
        stacked = row_factor.reshape(row_blocks, width, PW)
        pieces = []
        for offset in range(ratio):
            pieces.append(
                broadcast(as_sent(stacked), "frow", col_here + col_devs * offset).astype(
                    stacked.dtype
                )
            )
        col_factor = jnp.stack(pieces, axis=1).reshape(local.shape[1], PW)
        matrix = subtract_product(matrix, row_factor, col_factor)
        in_panel = (col_here >= col_first) & (col_here < col_first + panel_blocks)
        shift_cols = jnp.clip(col_here - col_first, 0, panel_blocks - 1) * width
        own_part = lax.dynamic_slice_in_dim(new_panel, shift_cols, width, axis=1)
        current = matrix[:, col_slot * width : (col_slot + 1) * width]
        matrix = matrix.at[:, col_slot * width : (col_slot + 1) * width].set(
            jnp.where(in_panel, own_part, current)
        )
    lower_part = global_rows[:, None] >= global_cols[None, :]
    result = jnp.where(lower_part, matrix, 0.0)
    return result[None, :, None, :]


def solution(mesh):
    return jax.shard_map(
        shards,
        mesh=mesh,
        in_specs=(
            P("frow", None, "fcol", None),
            P(("frow", "fcol"), None, None),
            P(("frow", "fcol"), None),
            P(("frow", "fcol"), None),
            P(("frow", "fcol"), None),
        ),
        out_specs=P("frow", None, "fcol", None),
        check_vma=False,
    )
```

profile of v0, /device:TPU:0, one launch (start us, length us, event | category | flops | bytes accessed | tf_op | source)
XLA Modules:
  0.0 1094.0 jit_solution(4737271812436628549)
XLA Ops:
  40.8 47.4 %all-to-all-done.2 = bf16[32,2,128,128]{3,2,1,0:T(8,128)(2,1)S(1)} async-done(((bf16[32,2,128,128]{3,2,1,0:T(8,128)(2,1)}), bf16[32,2,128,128]{3,2,1,0:T(8,128)(2,1)S(1)}, u32[]{:S(2)}, u32[]{:S(2)}) %all-to-all-start.2) | async-done | bytes 2097184 | tf_op jit(solution)/shard_map/all_to_all | solution.py:75
  93.4 15.0 %fusion.22 = f32[16,32,128,128]{3,1,2,0:T(8,128)} fusion(s32[16,32]{1,0:T(8,128)S(1)} %multiply_add_fusion, s32[64]{0:T(128)S(1)} %eq.97, bf16[8,8,128,128]{3,2,1,0:T(8,128)(2,1)S(1)} %bitcast.192), kind=kOutput, calls=%fused_computation.46 | convolution fusion | flops 1073774592 | bytes 35653888 | tf_op jit(solution)/shard_map/dot_general | solution.py:103
  108.4 74.5 %bitcast_add_fusion = f32[2048,4096]{1,0:T(8,128)} fusion(f32[256,8,32,128]{3,2,1,0:T(8,128)} %bitcast.174, f32[1,2048,1,4096]{3,2,1,0:T(1,128)} %param.16), kind=kLoop, calls=%fused_computation.10 | loop fusion | flops 8388608 | bytes 100663296 | tf_op jit(solution)/shard_map/add | solution.py:111
  185.0 22.2 %all-gather.5.cloned.1.call-done = bf16[2048,512]{1,0:T(8,128)(2,1)} async-done(((bf16[2048,128]{1,0:T(8,128)(2,1)}), bf16[2048,512]{1,0:T(8,128)(2,1)}) %all-gather.5.cloned.1.call-update) | async-done | bytes 2097168 | tf_op jit(solution)/shard_map/all_gather | solution.py:127
  213.5 36.0 %all-gather.7.cloned.1.call-done = bf16[1024,512]{1,0:T(8,128)(2,1)} async-done(((bf16[128,512]{1,0:T(8,128)(2,1)}), bf16[1024,512]{1,0:T(8,128)(2,1)}) %all-gather.7.cloned.1.call-update) | async-done | bytes 1048592 | tf_op jit(solution)/shard_map/all_gather | solution.py:131
  252.9 11.7 %cholesky.286 = f32[128,128]{1,0:T(8,128)S(1)} custom-call(f32[128,128]{1,0:T(8,128)S(1)} %cholesky.426), custom_call_target="Cholesky" | custom-call | tf_op jit(solution)/shard_map/jit(cholesky)/cholesky | solution.py:139
  264.8 9.8 custom-call.27
  275.3 11.7 %cholesky.305 = f32[128,128]{1,0:T(8,128)S(1)} custom-call(f32[128,128]{1,0:T(8,128)S(1)} %cholesky.430), custom_call_target="Cholesky" | custom-call | tf_op jit(solution)/shard_map/jit(cholesky)/cholesky | solution.py:139
  287.0 10.0 custom-call.28
  297.6 11.7 %cholesky.326 = f32[128,128]{1,0:T(8,128)S(1)} custom-call(f32[128,128]{1,0:T(8,128)S(1)} %cholesky.435), custom_call_target="Cholesky" | custom-call | tf_op jit(solution)/shard_map/jit(cholesky)/cholesky | solution.py:139
  309.4 9.8 custom-call.29
  319.8 12.1 %cholesky.343 = f32[128,128]{1,0:T(8,128)S(1)} custom-call(f32[128,128]{1,0:T(8,128)S(1)} %convolution_subtract_fusion.11), custom_call_target="Cholesky" | custom-call | tf_op jit(solution)/shard_map/jit(cholesky)/cholesky | solution.py:139
  336.9 8.2 while.6
  346.1 39.3 %custom-call.30 = f32[4,128,128]{1,2,0:T(8,128)S(1)} custom-call(f32[4,128,128]{2,1,0:T(8,128)S(1)} %get-tuple-element.47), custom_call_target="InvertDiagBlocksLowerTriangular" | custom-call | tf_op jit(solution)/shard_map/triangular_solve/custom-call.3 | solution.py:140
  407.6 8.9 gather_fusion.4
  420.4 141.8 %all-reduce.8.cloned.1.call-done = (bf16[16,1,128,512]{3,2,1,0:T(8,128)(2,1)}, bf16[16,1,128,512]{3,2,1,0:T(8,128)(2,1)}) async-done(((bf16[16,1,128,512]{3,2,1,0:T(8,128)(2,1)}, bf16[16,1,128,512]{3,2,1,0:T(8,128)(2,1)}), (bf16[16,1,128,512]{3,2,1,0:T(8,128)(2,1)}, bf16[16,1,128,512]{3,2,1,0:T(8,128)(2,1)})) %all-reduce.8.cloned.1.call-update) | async-done | bytes 4194320 | tf_op jit(solution)/shard_map/psum | solution.py:17
  565.0 34.7 %convolution_subtract_fusion.1 = f32[2048,4096]{1,0:T(8,128)} fusion(f32[2048,4096]{1,0:T(8,128)} %bitcast_add_fusion, bf16[4096,512]{1,0:T(8,128)(2,1)S(1)} %bitcast.185, pred[2048]{0:T(1024)(128)(4,1)S(1)} %get-tuple-element.116, f32[2048,128]{1,0:T(8,128)S(1)} %copy-done.7, f32[2048,128]{1,0:T(8,128)S(1)} %copy-done.3, f32[2048,128]{1,0:T(8,128)S(1)} %fusion.84, ...), kind=kOutput, calls=%fused_computation.13 | convolution fusion | flops 51552190464 | bytes 75499520 | tf_op jit(solution)/shard_map/dot_general | solution.py:36
  607.0 21.9 %all-gather.9.cloned.1.call-done = bf16[2048,512]{1,0:T(8,128)(2,1)} async-done(((bf16[2048,128]{1,0:T(8,128)(2,1)}), bf16[2048,512]{1,0:T(8,128)(2,1)}) %all-gather.9.cloned.1.call-update) | async-done | bytes 2097168 | tf_op jit(solution)/shard_map/all_gather | solution.py:127
  635.2 35.9 %all-gather.11.cloned.1.call-done = bf16[1024,512]{1,0:T(8,128)(2,1)} async-done(((bf16[128,512]{1,0:T(8,128)(2,1)}), bf16[1024,512]{1,0:T(8,128)(2,1)}) %all-gather.11.cloned.1.call-update) | async-done | bytes 1048592 | tf_op jit(solution)/shard_map/all_gather | solution.py:131
  673.6 11.7 %cholesky.358 = f32[128,128]{1,0:T(8,128)S(1)} custom-call(f32[128,128]{1,0:T(8,128)S(1)} %cholesky.439), custom_call_target="Cholesky" | custom-call | tf_op jit(solution)/shard_map/jit(cholesky)/cholesky | solution.py:139
  685.4 9.8 custom-call.31
  695.9 12.1 %cholesky.377 = f32[128,128]{1,0:T(8,128)S(1)} custom-call(f32[128,128]{1,0:T(8,128)S(1)} %cholesky.443), custom_call_target="Cholesky" | custom-call | tf_op jit(solution)/shard_map/jit(cholesky)/cholesky | solution.py:139
  708.1 9.8 custom-call.32
  718.5 11.7 %cholesky.398 = f32[128,128]{1,0:T(8,128)S(1)} custom-call(f32[128,128]{1,0:T(8,128)S(1)} %cholesky.448), custom_call_target="Cholesky" | custom-call | tf_op jit(solution)/shard_map/jit(cholesky)/cholesky | solution.py:139
  730.3 9.8 custom-call.33
  740.7 11.9 %cholesky.415 = f32[128,128]{1,0:T(8,128)S(1)} custom-call(f32[128,128]{1,0:T(8,128)S(1)} %convolution_subtract_fusion.10), custom_call_target="Cholesky" | custom-call | tf_op jit(solution)/shard_map/jit(cholesky)/cholesky | solution.py:139
  766.8 39.3 %custom-call.34 = f32[4,128,128]{1,2,0:T(8,128)S(1)} custom-call(f32[4,128,128]{2,1,0:T(8,128)S(1)} %get-tuple-element.48), custom_call_target="InvertDiagBlocksLowerTriangular" | custom-call | tf_op jit(solution)/shard_map/triangular_solve/custom-call.3 | solution.py:140
  828.0 9.1 gather_fusion.5
  840.8 142.0 %all-reduce.6.cloned.1.call-done = (bf16[16,1,128,512]{3,2,1,0:T(8,128)(2,1)}, bf16[16,1,128,512]{3,2,1,0:T(8,128)(2,1)}) async-done(((bf16[16,1,128,512]{3,2,1,0:T(8,128)(2,1)}, bf16[16,1,128,512]{3,2,1,0:T(8,128)(2,1)}), (bf16[16,1,128,512]{3,2,1,0:T(8,128)(2,1)}, bf16[16,1,128,512]{3,2,1,0:T(8,128)(2,1)})) %all-reduce.6.cloned.1.call-update) | async-done | bytes 4194320 | tf_op jit(solution)/shard_map/psum | solution.py:17
  985.6 34.7 %convolution_subtract_fusion = f32[2048,4096]{1,0:T(8,128)} fusion(f32[2048,4096]{1,0:T(8,128)} %fusion.43, bf16[4096,512]{1,0:T(8,128)(2,1)S(1)} %bitcast.186, pred[2048]{0:T(1024)(128)(4,1)S(1)} %get-tuple-element.115, f32[2048,128]{1,0:T(8,128)S(1)} %copy-done.9, f32[2048,128]{1,0:T(8,128)S(1)} %copy-done.5, f32[2048,128]{1,0:T(8,128)S(1)} %fusion.78, ...), kind=kOutput, calls=%fused_computation.12 | convolution fusion | flops 51552190464 | bytes 75499520 | tf_op jit(solution)/shard_map/dot_general | solution.py:36
  1025.4 23.4 %select_bitcast_fusion = f32[1,2048,1,4096]{3,1,2,0:T(8,128)} fusion(f32[2048,4096]{1,0:T(8,128)} %fusion.44, s32[4096]{0:T(1024)S(1)} %fusion.105, s32[2048]{0:T(1024)S(1)} %get-tuple-element.111), kind=kLoop, calls=%fused_computation.11 | loop fusion | flops 16777216 | bytes 67133440 | tf_op jit(solution)/shard_map/broadcast_in_dim | solution.py:167
  1048.9 38.0 %copy.110 = f32[1,2048,1,4096]{3,2,1,0:T(1,128)} copy(f32[1,2048,1,4096]{3,1,2,0:T(8,128)} %select_bitcast_fusion) | data formatting | bytes 67108864 | tf_op jit(solution)/shard_map/broadcast_in_dim | solution.py:167
  (191 shorter events, 164.3 us)
Async XLA Ops:
  6.5 14.5 %copy-start = (bf16[64,128,128]{2,1,0:T(8,128)(2,1)S(1)}, bf16[64,128,128]{2,1,0:T(8,128)(2,1)}, u32[]{:S(2)}) copy-start(bf16[64,128,128]{2,1,0:T(8,128)(2,1)} %param.17) | copy-start | bytes 6291460
  10.0 14.4 %all-to-all-start = ((s32[32,1,2]{2,1,0:T(1,128)}), s32[32,1,2]{2,1,0:T(1,128)S(1)}, u32[]{:S(2)}, u32[]{:S(2)}) async-start(s32[32,1,2]{2,1,0:T(1,128)} %bitcast.4), calls=%async_computation | async-start | bytes 32768 | tf_op jit(solution)/shard_map/all_to_all | solution.py:89
  24.4 12.1 %all-to-all-start.1 = ((s32[32,2,2,128]{3,1,2,0:T(2,128)}), s32[32,2,2,128]{3,1,2,0:T(2,128)S(1)}, u32[]{:S(2)}, u32[]{:S(2)}) async-start(s32[32,2,2,128]{3,1,2,0:T(2,128)} %pad_add_fusion), calls=%async_computation.1 | async-start | bytes 131072 | tf_op jit(solution)/shard_map/all_to_all | solution.py:82
  36.5 51.7 %all-to-all-start.2 = ((bf16[32,2,128,128]{3,2,1,0:T(8,128)(2,1)}), bf16[32,2,128,128]{3,2,1,0:T(8,128)(2,1)S(1)}, u32[]{:S(2)}, u32[]{:S(2)}) async-start(bf16[32,2,128,128]{3,2,1,0:T(8,128)(2,1)} %select_select_fusion), calls=%async_computation.2 | async-start | bytes 4194304 | tf_op jit(solution)/shard_map/all_to_all | solution.py:75
  39.3 167.9 %all-gather.5.cloned.1.call-start = ((), (), s32[]{:S(2)}) async-start(), calls=%async_computation.3 | async-start | bytes 2621440 | tf_op jit(solution)/shard_map/all_gather | solution.py:127
  88.2 1.3 copy-start.12
  184.9 64.6 %all-gather.7.cloned.1.call-start = ((), (), s32[]{:S(2)}) async-start(), calls=%async_computation.4 | async-start | bytes 1179648 | tf_op jit(solution)/shard_map/all_gather | solution.py:131
  208.8 353.5 %all-reduce.8.cloned.1.call-start = ((), (), s32[]{:S(2)}) async-start(), calls=%async_computation.8 | async-start | bytes 8388608 | tf_op jit(solution)/shard_map/psum | solution.py:17
  345.1 1.0 copy-start.11
  398.5 8.2 copy-start.2
  404.2 2.5 copy-start.6
  406.7 222.3 %all-gather.9.cloned.1.call-start = ((), (), s32[]{:S(2)}) async-start(), calls=%async_computation.5 | async-start | bytes 2621440 | tf_op jit(solution)/shard_map/all_gather | solution.py:127
  562.2 2.8 copy-start.3
  562.2 2.8 copy-start.7
  606.9 64.1 %all-gather.11.cloned.1.call-start = ((), (), s32[]{:S(2)}) async-start(), calls=%async_computation.6 | async-start | bytes 1179648 | tf_op jit(solution)/shard_map/all_gather | solution.py:131
  630.5 352.3 %all-reduce.6.cloned.1.call-start = ((), (), s32[]{:S(2)}) async-start(), calls=%async_computation.7 | async-start | bytes 8388608 | tf_op jit(solution)/shard_map/psum | solution.py:17
  671.1 1.6 copy-start.13
  765.9 1.0 copy-start.10
  819.2 8.1 copy-start.4
  824.9 2.4 copy-start.8
  982.8 2.8 copy-start.5
  982.8 2.8 copy-start.9
  1048.9 38.0 %copy-start.1 = (bf16[64,128,128]{2,1,0:T(8,128)(2,1)S(1)}, bf16[64,128,128]{2,1,0:T(8,128)(2,1)}, u32[]{:S(2)}) copy-start(bf16[64,128,128]{2,1,0:T(8,128)(2,1)} %param.17) | copy-start | bytes 6291460
Sparse Core Ops, SparseCore 0:
  185.1 22.0 all-gather.4
  209.3 40.1 all-gather.6
  406.8 155.4 all-reduce.7
  607.1 21.8 all-gather.8
  630.9 40.1 all-gather.10
  827.4 155.3 all-reduce.5
where the time goes:
time: 1100 us; the launch traced here: 1090 us
  waiting for transfers between devices  453 us (41%)
  other arithmetic  385 us (35%)
  matrix products  129 us (12%)
  local copies, waits for them, and re-layouts  92.8 us (8%)
  between operations  19.5 us (2%)
  starting transfers between devices  15.3 us (1%)
    psum x2, waiting for transfers between devices, broadcast(): return lax.psum(block, axis)  284 us
    another operation x29, other arithmetic, shards(): factor = jnp.linalg.cholesky(symmetric)  159 us
    another operation x7, other arithmetic, shards(): lax.linalg.triangular_solve(factor, panel, left_side=False, lower=True, t...  86.7 us
    add x1, other arithmetic, shards(): matrix = local + added  74.5 us
    all_gather x2, waiting for transfers between devices, shards(): lax.all_gather(panel[row_slot * width:(row_slot + 1) * width].astype(jnp....  72 us
    dot_general x2, matrix products, subtract_product(): jnp.dot(row_factor, col_factor.T, precision=lax.Precision.HIGHEST, prefer...  69.3 us
    all_to_all x1, waiting for transfers between devices, shards(): lax.all_to_all(send_tiles.reshape(owners, CAP, width, width), ('frow', 'f...  47.4 us
    all_gather x2, waiting for transfers between devices, shards(): lax.all_gather(own_column.astype(jnp.bfloat16), 'fcol', axis=1, tiled=True)  44.1 us
  transfers between devices with their start and end apart: 9, of which 9 were waited for; matrix products, arithmetic and copies ran while one was open for 4% of the time, Pallas kernels for 0%

commit v1 on v0

v1 whole, which is shorter than its diff:
```python
import functools

import jax
import jax.numpy as jnp
from jax import lax
from jax.experimental import pallas as pl
from jax.experimental.pallas import tpu as pltpu
from jax.sharding import PartitionSpec as P

PW = 512
NPANEL = 2
CAP = 2
NB = 128
GROUP = 8
WIDE = PW * NPANEL
BLOCKS = WIDE // NB
HIGHEST = lax.Precision.HIGHEST


def dot_tn(a, b):
    return lax.dot_general(
        a, b, (((0,), (0,)), ((), ())), precision=HIGHEST, preferred_element_type=jnp.float32
    )


def factor_block(t_ref):
    lane = lax.broadcasted_iota(jnp.int32, (GROUP, NB), 1)
    sub = lax.broadcasted_iota(jnp.int32, (GROUP, NB), 0)
    for first in range(0, NB, GROUP):
        rows = t_ref[first : first + GROUP, :]
        w = [rows[k : k + 1, :] for k in range(GROUP)]
        s = {}
        for a in range(GROUP):
            for b in range(a, GROUP):
                s[a, b] = jnp.broadcast_to(rows[a : a + 1, first + b : first + b + 1], (1, NB))
        for k in range(GROUP):
            scale = lax.rsqrt(s[k, k])
            scale2 = jnp.concatenate([scale, scale], axis=1)
            w[k] = w[k] * scale2
            coef = {m: s[k, m] * scale for m in range(k + 1, GROUP)}
            for m in range(k + 1, GROUP):
                for n in range(m, GROUP):
                    s[m, n] = s[m, n] - coef[m] * coef[n]
                w[m] = w[m] - jnp.concatenate([coef[m], coef[m]], axis=1) * w[k]
        done = jnp.concatenate(w, axis=0)
        upper = jnp.where(lane >= first + sub, done[:, :NB], 0.0)
        done = jnp.concatenate([upper, done[:, NB:]], axis=1)
        t_ref[first : first + GROUP, :] = done
        if first + GROUP < NB:
            change = dot_tn(upper, done)
            t_ref[first + GROUP :, :] -= change[first + GROUP :, :]


def factor_kernel(d_ref, m_ref, u_ref, t_ref, p_ref):
    m_ref[...] = d_ref[...]
    r = lax.broadcasted_iota(jnp.int32, (NB, NB), 0)
    c = lax.broadcasted_iota(jnp.int32, (NB, NB), 1)

    def step(k, _):
        here = pl.ds(pl.multiple_of(k * NB, NB), NB)
        t_ref[:, :NB] = m_ref[here, here]
        t_ref[:, NB:] = jnp.where(r == c, 1.0, 0.0)
        factor_block(t_ref)
        u_ref[here, :] = t_ref[:, :NB]
        inverse = t_ref[:, NB:]
        p_ref[...] = jnp.dot(
            inverse, m_ref[here, :], precision=HIGHEST, preferred_element_type=jnp.float32
        )
        p_ref[:, here] = inverse
        m_ref[here, :] = p_ref[...]

        def below(i, _):
            there = pl.ds(pl.multiple_of(i * NB, NB), NB)
            m_ref[there, here] = jnp.zeros((NB, NB), jnp.float32)
            m_ref[there, :] -= dot_tn(p_ref[:, there], p_ref[...])
            return 0

        lax.fori_loop(k + 1, BLOCKS, below, 0)
        return 0

    lax.fori_loop(0, BLOCKS, step, 0)


def factor_diagonal(diag):
    return pl.pallas_call(
        factor_kernel,
        out_shape=(
            jax.ShapeDtypeStruct((WIDE, WIDE), jnp.float32),
            jax.ShapeDtypeStruct((WIDE, NB), jnp.float32),
        ),
        in_specs=[pl.BlockSpec(memory_space=pltpu.VMEM)],
        out_specs=(
            pl.BlockSpec(memory_space=pltpu.VMEM),
            pl.BlockSpec(memory_space=pltpu.VMEM),
        ),
        scratch_shapes=[
            pltpu.VMEM((NB, 2 * NB), jnp.float32),
            pltpu.VMEM((NB, WIDE), jnp.float32),
        ],
        compiler_params=pltpu.CompilerParams(vmem_limit_bytes=32 * 1024 * 1024),
        cost_estimate=pl.CostEstimate(
            flops=20 * WIDE**3, bytes_accessed=WIDE * WIDE * 8, transcendentals=WIDE
        ),
    )(diag)


STEP = 2
CHUNK = 4


def update_kernel(
    row_devs, col_devs, nc, own, ids, pos, front_ref, rowf_ref, colf_ref, panel_ref, tiles_ref, out_ref
):
    g = pl.program_id(0)
    row_here, col_here = pos[0], pos[1]
    r = lax.broadcasted_iota(jnp.int32, (NB, NB), 0)
    c = lax.broadcasted_iota(jnp.int32, (NB, NB), 1)

    def place(b, col):
        return pl.ds(b * NB * nc + col, NB, stride=nc)

    last_row = (g * STEP + STEP - 1) * row_devs + row_here
    for chunk in range(0, nc, CHUNK):
        active = chunk * col_devs + col_here <= last_row

        @pl.when(active)
        def _(chunk=chunk):
            product = lax.dot_general(
                rowf_ref[...],
                colf_ref[chunk * NB : (chunk + CHUNK) * NB, :],
                (((1,), (1,)), ((), ())),
                preferred_element_type=jnp.float32,
            )
            for b in range(STEP):
                row_block = (g * STEP + b) * row_devs + row_here
                for cc in range(CHUNK):
                    col = chunk + cc
                    if col < own:
                        out_ref[place(b, col), :] = panel_ref[
                            b * NB : (b + 1) * NB, col * NB : (col + 1) * NB
                        ]
                    else:
                        gap = (row_block - (col * col_devs + col_here)) * NB
                        value = (
                            front_ref[place(b, col), :]
                            - product[b * NB : (b + 1) * NB, cc * NB : (cc + 1) * NB]
                        )
                        out_ref[place(b, col), :] = jnp.where(r + gap >= c, value, 0.0)

        @pl.when(jnp.logical_not(active))
        def _(chunk=chunk):
            for b in range(STEP):
                for cc in range(CHUNK):
                    out_ref[place(b, chunk + cc), :] = jnp.zeros((NB, NB), jnp.float32)

    def add_tile(t, _):
        block = ids[t]
        br = block // nc
        bc = block % nc

        @pl.when((br // STEP == g) & (bc >= own))
        def _():
            gap = (br * row_devs + row_here - (bc * col_devs + col_here)) * NB
            tile = tiles_ref[t].astype(jnp.float32)
            where = place(br % STEP, bc)
            out_ref[where, :] += jnp.where(r + gap >= c, tile, 0.0)

        return 0

    lax.fori_loop(0, tiles_ref.shape[0], add_tile, 0)


def update(front, rowf, colf, panel, tiles, ids, pos, row_devs, col_devs):
    rows, cols = rowf.shape[0], colf.shape[0]
    nc = cols // NB
    own = panel.shape[1] // NB
    height = STEP * NB
    return pl.pallas_call(
        functools.partial(update_kernel, row_devs, col_devs, nc, own),
        out_shape=jax.ShapeDtypeStruct((rows * nc, NB), jnp.float32),
        grid_spec=pltpu.PrefetchScalarGridSpec(
            num_scalar_prefetch=2,
            grid=(rows // height,),
            in_specs=[
                pl.BlockSpec((height * nc, NB), lambda g, *_: (g, 0)),
                pl.BlockSpec((height, WIDE), lambda g, *_: (g, 0)),
                pl.BlockSpec(memory_space=pltpu.VMEM),
                pl.BlockSpec((height, own * NB), lambda g, *_: (g, 0)),
                pl.BlockSpec(memory_space=pltpu.VMEM),
            ],
            out_specs=pl.BlockSpec((height * nc, NB), lambda g, *_: (g, 0)),
        ),
        compiler_params=pltpu.CompilerParams(vmem_limit_bytes=48 * 1024 * 1024),
        cost_estimate=pl.CostEstimate(
            flops=rows * cols * WIDE, bytes_accessed=rows * cols * 8, transcendentals=0
        ),
    )(ids, pos, front, rowf, colf, panel, tiles)


def place_tiles(tile_block, perm_block):
    width = tile_block.shape[-1]
    positions = jnp.arange(width, dtype=jnp.int32)
    row_onehot = (perm_block[:, 0, None, :] == positions[:, None]).astype(jnp.bfloat16)
    col_onehot = (perm_block[:, 1, None, :] == positions[:, None]).astype(jnp.bfloat16)
    moved = jnp.einsum(
        "axi,aij->axj", row_onehot, tile_block, preferred_element_type=jnp.float32
    ).astype(jnp.bfloat16)
    return jnp.einsum(
        "axj,ayj->axy", moved, col_onehot, preferred_element_type=jnp.float32
    ).astype(jnp.bfloat16)


def exchange(x):
    return lax.all_to_all(x, ("frow", "fcol"), split_axis=0, concat_axis=0, tiled=True)


def shards(front_orig, child_tiles, tile_target, tile_rows, tile_cols):
    row_devs = lax.axis_size("frow")
    col_devs = lax.axis_size("fcol")
    owners = row_devs * col_devs
    row_here = lax.axis_index("frow")
    col_here = lax.axis_index("fcol")
    held = child_tiles.shape[0]
    slot_count = owners * CAP
    owner_of = tile_target[:, 0]
    block_of = tile_target[:, 1]
    tile_order = jnp.arange(held, dtype=jnp.int32)
    same_owner = owner_of[:, None] == owner_of[None, :]
    earlier = tile_order[None, :] < tile_order[:, None]
    rank_of = jnp.sum(jnp.where(same_owner & earlier, 1, 0), axis=1).astype(jnp.int32)
    slot_of = owner_of * CAP + rank_of
    slot_match = slot_of[None, :] == jnp.arange(slot_count, dtype=jnp.int32)[:, None]
    source_tile = jnp.sum(jnp.where(slot_match, tile_order[None, :], 0), axis=1)
    lists = jnp.stack(
        [tile_rows, tile_cols, jnp.broadcast_to(block_of[:, None], tile_rows.shape)], axis=1
    )
    lists_in = exchange(jnp.take(lists, source_tile, axis=0).reshape(owners, CAP, 3, NB))
    tiles_in = exchange(jnp.take(child_tiles, source_tile, axis=0).reshape(owners, CAP, NB, NB))
    lists_in = lists_in.reshape(slot_count, 3, NB)
    ids = lists_in[:, 2, 0]
    placed = place_tiles(tiles_in.reshape(slot_count, NB, NB), lists_in[:, :2])

    rows, cols = front_orig.shape[1], front_orig.shape[3]
    lrb, nc = rows // NB, cols // NB
    own = BLOCKS // col_devs
    ratio = row_devs // col_devs

    panel_ids = (jnp.arange(lrb)[:, None] * nc + jnp.arange(own)[None, :]).reshape(-1, 1)
    panel_onehot = (ids[None, :] == panel_ids).astype(jnp.bfloat16)
    added = jnp.dot(
        panel_onehot, placed.reshape(slot_count, NB * NB), preferred_element_type=jnp.float32
    )
    added = added.reshape(lrb, own, NB, NB).transpose(0, 2, 1, 3).reshape(rows, own * NB)
    own_panel = (front_orig[0, :, 0, : own * NB] + added).astype(jnp.bfloat16)

    corner = lax.all_gather(own_panel[:NB], ("frow", "fcol"), axis=0, tiled=False)
    corner = corner.reshape(row_devs, col_devs, NB, own, NB)[:BLOCKS]
    diag = corner.transpose(0, 2, 3, 1, 4).reshape(WIDE, WIDE).astype(jnp.float32)
    diag = jnp.tril(diag) + jnp.tril(diag, -1).T

    route = []
    for p in range(row_devs):
        for q in range(col_devs):
            route.append((p * col_devs + q, (q * ratio + p // col_devs) * col_devs + p % col_devs))
    turned = lax.ppermute(own_panel, ("frow", "fcol"), route)
    col_raw = lax.all_gather(turned, "frow", axis=0, tiled=False)
    col_raw = col_raw.reshape(col_devs, ratio, lrb, NB, own, NB)
    col_raw = col_raw.transpose(2, 1, 3, 4, 0, 5).reshape(cols, WIDE)
    row_raw = lax.all_gather(own_panel, "fcol", axis=0, tiled=False)
    row_raw = row_raw.reshape(col_devs, rows, own, NB).transpose(1, 2, 0, 3).reshape(rows, WIDE)

    packed, diag_upper = factor_diagonal(diag)
    inverse = jnp.tril(packed).astype(jnp.bfloat16)

    def solve(raw, dtype):
        return lax.dot_general(
            raw, inverse, (((1,), (1,)), ((), ())), preferred_element_type=jnp.float32
        ).astype(dtype)

    rowf = solve(row_raw, jnp.bfloat16)
    colf = solve(col_raw, jnp.bfloat16)
    own_inverse = lax.dynamic_index_in_dim(
        inverse.reshape(own, col_devs, NB, WIDE), col_here, axis=1, keepdims=False
    ).reshape(own * NB, WIDE)
    solved = lax.dot_general(
        row_raw, own_inverse, (((1,), (1,)), ((), ())), preferred_element_type=jnp.float32
    )
    block = jnp.minimum(row_here, BLOCKS - 1)
    above = lax.dynamic_slice(packed, (0, block * NB), (WIDE, NB))
    on = lax.dynamic_slice(diag_upper, (block * NB, 0), (NB, NB)).T
    corner_blocks = []
    for j in range(own):
        col_block = col_here + j * col_devs
        left = lax.dynamic_slice(above, (col_block * NB, 0), (NB, NB)).T
        corner_blocks.append(
            jnp.where(col_block < block, left, jnp.where(col_block == block, on, 0.0))
        )
    corner_own = jnp.where(
        row_here < BLOCKS, jnp.concatenate(corner_blocks, axis=1), solved[:NB]
    )
    panel = jnp.concatenate([corner_own, solved[NB:]], axis=0)

    out = update(
        front_orig.reshape(rows * nc, NB),
        rowf,
        colf,
        panel,
        placed,
        ids,
        jnp.stack([row_here, col_here]).astype(jnp.int32),
        row_devs,
        col_devs,
    )
    return out.reshape(front_orig.shape)


def solution(mesh):
    return jax.shard_map(
        shards,
        mesh=mesh,
        in_specs=(
            P("frow", None, "fcol", None),
            P(("frow", "fcol"), None, None),
            P(("frow", "fcol"), None),
            P(("frow", "fcol"), None),
            P(("frow", "fcol"), None),
        ),
        out_specs=P("frow", None, "fcol", None),
        check_vma=False,
    )
```

time: 1100 us -> 471 us (0.43)
  other arithmetic: 385 us -> 23.6 us
  waiting for transfers between devices: 453 us -> 127 us
  Pallas kernels: 0 us -> 160 us
  matrix products: 129 us -> 29 us
    psum x2 -> x0, waiting for transfers between devices: 284 us -> none  [broadcast(): return lax.psum(block, axis)]
    another operation x41 -> x2, other arithmetic: 253 us -> 0.94 us  [the longest x1 0.87 us: shards(): jnp.stack([tile_rows, tile_cols, jnp.broadcast_to(block_of[:, None], tile...]
    pallas_call x0 -> x2, Pallas kernels: none -> 160 us  [the longest x1 85.8 us: factor_diagonal(): pl.pallas_call(factor_kernel, out_shape=(jax.ShapeDtypeStruct((WIDE, WIDE...]
    add x6 -> x3, other arithmetic: 76 us -> 5.13 us  [the longest x2 5.13 us: shards(): diag = jnp.tril(diag) + jnp.tril(diag, -1).T]
    dot_general x4 -> x5, matrix products: 88.2 us -> 29 us  [the longest x2 21 us: solve(): lax.dot_general(raw, inverse, (((1,), (1,)), ((), ())), preferred_element...]
    another operation x26 -> x0, matrix products: 40.5 us -> none  [the longest x14 36.7 us: shards(): lax.linalg.triangular_solve(factor, panel, left_side=False, lower=True, t...]
    broadcast_in_dim x2 -> x0, local copies, waits for them, and re-layouts: 38.2 us -> none  [the longest x1 38 us: shards(): return result[None, :, None, :]]
    all_gather x4 -> x3, waiting for transfers between devices: 116 us -> 82 us  [the longest x1 67.4 us: shards(): lax.all_gather(own_panel[:NB], ('frow', 'fcol'), axis=0, tiled=False)]
  transfers between devices with their start and end apart: 9 -> 6, of which waited for: 9 -> 4; matrix products, arithmetic and copies ran while one was open for 4% -> 16% of each run, Pallas kernels for 0% -> 19%
where the time goes in v1:
time: 471 us; the launch traced here: 464 us
  Pallas kernels  160 us (34%)
  waiting for transfers between devices  127 us (27%)
  local copies, waits for them, and re-layouts  98.6 us (21%)
  matrix products  29 us (6%)
  other arithmetic  23.6 us (5%)
  between operations  13.8 us (3%)
  starting transfers between devices  11.8 us (3%)
    pallas_call x1, Pallas kernels, factor_diagonal(): pl.pallas_call(factor_kernel, out_shape=(jax.ShapeDtypeStruct((WIDE, WIDE...  85.8 us
    pallas_call x1, Pallas kernels, update(): pl.pallas_call(functools.partial(update_kernel, row_devs, col_devs, nc, o...  74.1 us
    all_gather x1, waiting for transfers between devices, shards(): lax.all_gather(own_panel[:NB], ('frow', 'fcol'), axis=0, tiled=False)  67.4 us
    all_to_all x2, waiting for transfers between devices, exchange(): lax.all_to_all(x, ('frow', 'fcol'), split_axis=0, concat_axis=0, tiled=True)  45.1 us
    unnamed x27, local copies, waits for them, and re-layouts  21.4 us
    dot_general x2, matrix products, solve(): lax.dot_general(raw, inverse, (((1,), (1,)), ((), ())), preferred_element...  21 us
    all_gather x1, waiting for transfers between devices, shards(): col_raw = lax.all_gather(turned, 'frow', axis=0, tiled=False)  14.6 us
    reshape x1, local copies, waits for them, and re-layouts, shards(): col_raw = col_raw.transpose(2, 1, 3, 4, 0, 5).reshape(cols, WIDE)  14.2 us
  transfers between devices with their start and end apart: 6, of which 4 were waited for; matrix products, arithmetic and copies ran while one was open for 16% of the time, Pallas kernels for 19%

profile of v1, /device:TPU:0, one launch (start us, length us, event | category | flops | bytes accessed | tf_op | source)
XLA Modules:
  0.0 464.0 jit_solution(7517601883328354722)
XLA Ops:
  10.9 7.3 %all-to-all-start = ((s32[32,2,3,128]{3,1,2,0:T(2,128)}), s32[32,2,3,128]{3,1,2,0:T(2,128)S(1)}, u32[]{:S(2)}, u32[]{:S(2)}) async-start(s32[32,2,3,128]{3,1,2,0:T(2,128)} %copy_select_fusion), calls=%async_computation | async-start | bytes 196608 | tf_op jit(solution)/shard_map/all_to_all | solution.py:214
  20.4 3.2 broadcast_select_fusion
  23.5 2.5 all-to-all-done
  26.0 3.5 all-to-all-start.1
  31.1 4.5 copy.99
  35.8 42.6 %all-to-all-done.1 = bf16[32,2,128,128]{3,2,1,0:T(8,128)(2,1)} async-done(((bf16[32,2,128,128]{3,2,1,0:T(8,128)(2,1)}), bf16[32,2,128,128]{3,2,1,0:T(8,128)(2,1)}, u32[]{:S(2)}, u32[]{:S(2)}) %all-to-all-start.1) | async-done | bytes 2097184 | tf_op jit(solution)/shard_map/all_to_all | solution.py:214
  78.4 3.9 fusion.12.tiles_ref
  82.2 2.8 fusion.15
  85.0 3.3 copy.84
  88.4 2.9 fusion.4
  92.4 2.8 reshape.140
  100.5 67.4 %all-gather.8.cloned.1.call-done = bf16[4096,256]{0,1:T(8,128)(2,1)} async-done(((bf16[128,256]{0,1:T(8,128)(2,1)}), bf16[4096,256]{0,1:T(8,128)(2,1)}) %all-gather.8.cloned.1.call-update) | async-done | bytes 2097168 | tf_op jit(solution)/shard_map/all_gather | solution.py:256
  167.9 6.1 %reshape.150 = f32[8,4,128,2,128]{2,1,0,4,3:T(4,128)} reshape(bf16[4096,256]{0,1:T(8,128)(2,1)} %all-gather.8.cloned.1.call-done) | data formatting | bytes 6291456 | tf_op jit(solution)/shard_map/convert_element_type | solution.py:258
  174.0 2.9 copy.89
  178.9 2.8 bitcast_select_fusion.1
  181.7 5.3 %copy.90 = f32[1024,1024]{1,0:T(8,128)} copy(f32[1024,1024]{0,1:T(8,128)} %bitcast_select_fusion.1) | data formatting | bytes 8388608 | tf_op jit(solution)/shard_map/jit(tril)/select_n | solution.py:259
  187.0 5.1 %fusion.1.d_ref = f32[1024,1024]{1,0:T(8,128)S(1)} fusion(f32[1024,1024]{1,0:T(8,128)} %copy.90, f32[128,8,8,128]{3,2,1,0:T(8,128)} %bitcast.114, s32[1024]{0:T(1024)S(1)} %iota_add_fusion), kind=kLoop, calls=%fused_computation.6 | loop fusion | flops 3145728 | bytes 12587008 | tf_op jit(solution)/shard_map/add | solution.py:259
  192.1 85.8 %shard_map.55 = (f32[1024,1024]{1,0:T(8,128)S(1)}, f32[1024,128]{1,0:T(8,128)S(1)}) custom-call(f32[1024,1024]{1,0:T(8,128)S(1)} %fusion.1.d_ref), custom_call_target="tpu_custom_call" | custom-call | flops 21474836480 | bytes 8388608 | tf_op jit(solution)/shard_map/pallas_call | solution.py:85
  280.0 5.3 %copy.91 = f32[1024,1024]{0,1:T(8,128)} copy(f32[1024,1024]{1,0:T(8,128)} %copy-done.5) | data formatting | bytes 8388608 | tf_op jit(solution)/shard_map/pallas_call | solution.py:85
  286.3 2.5 select_convert_fusion
  288.8 2.7 reshape.146
  291.5 2.7 constant_dynamic-slice_fusion
  294.2 2.3 copy.100
  297.6 6.4 %copy.86 = bf16[4,2048,256]{1,2,0:T(8,128)(2,1)} copy(bf16[4,2048,256]{2,1,0:T(8,128)(2,1)} %all-gather.6.cloned.1.call-done) | data formatting | bytes 8388608 | tf_op jit(solution)/shard_map/all_gather | solution.py:269
  304.0 2.8 copy.87
  309.8 6.2 %convolution_convert_fusion.1.rowf_ref = bf16[2048,1024]{1,0:T(8,128)(2,1)} fusion(bf16[2048,1024]{0,1:T(8,128)(2,1)S(1)} %bitcast.122, bf16[1024,1024]{0,1:T(8,128)(2,1)S(1)} %select_convert_fusion), kind=kOutput, calls=%fused_computation.14 | convolution fusion | flops 4297064448 | bytes 10485760 | tf_op jit(solution)/shard_map/dot_general | solution.py:276
  316.0 14.6 %all-gather.10.cloned.1.call-done = bf16[16384,256]{0,1:T(8,128)(2,1)} async-done(((bf16[2048,256]{0,1:T(8,128)(2,1)}), bf16[16384,256]{0,1:T(8,128)(2,1)}) %all-gather.10.cloned.1.call-update) | async-done | bytes 8388624 | tf_op jit(solution)/shard_map/all_gather | solution.py:266
  330.6 9.4 %copy.105 = bf16[32,8,128,128]{3,2,1,0:T(8,128)(2,1)} copy(bf16[32,8,128,128]{3,1,2,0:T(8,128)(2,1)} %bitcast.120) | data formatting | bytes 16777216
  340.0 13.9 %copy.92 = bf16[4,2,16,128,2,128]{5,0,4,3,1,2:T(4,128)(2,1)} copy(bf16[4,2,16,128,2,128]{3,2,1,0,5,4:T(8,128)(2,1)} %bitcast.115) | data formatting | bytes 16777216 | tf_op jit(solution)/shard_map/reshape | solution.py:267
  353.9 14.2 %reshape.145 = bf16[4096,1024]{1,0:T(8,128)(2,1)} reshape(bf16[16,2,128,2,4,128]{5,4,3,2,1,0:T(4,128)(2,1)} %bitcast.116) | data formatting | bytes 16777216 | tf_op jit(solution)/shard_map/reshape | solution.py:268
  368.1 14.7 %convolution_convert_fusion.colf_ref = bf16[4096,1024]{1,0:T(8,128)(2,1)} fusion(bf16[4096,1024]{1,0:T(8,128)(2,1)} %reshape.145, bf16[1024,1024]{0,1:T(8,128)(2,1)S(1)} %select_convert_fusion), kind=kOutput, calls=%fused_computation.2 | convolution fusion | flops 8594128896 | bytes 18874368 | tf_op jit(solution)/shard_map/dot_general | solution.py:276
  382.9 74.1 %shard_map.56 = f32[65536,128]{1,0:T(8,128)} custom-call(s32[64]{0:T(128)S(1)} %slice_reduce_fusion.ids, s32[2]{0:T(128)S(1)} %pad_add_fusion.1.pos, f32[65536,128]{1,0:T(8,128)} %bitcast.112, bf16[2048,1024]{1,0:T(8,128)(2,1)} %convolution_convert_fusion.1.rowf_ref, bf16[4096,1024]{1,0:T(8,128)(2,1)} %convolution_convert_fusion.colf_ref, ...), custom_call_target="tpu_custom_call" | custom-call | flops 8589934592 | bytes 67108864 | tf_op jit(solution)/shard_map/pallas_call | solution.py:178
  (64 shorter events, 23.5 us)
Async XLA Ops:
  6.5 11.7 %copy-start = (bf16[64,128,128]{2,1,0:T(8,128)(2,1)S(1)}, bf16[64,128,128]{2,1,0:T(8,128)(2,1)}, u32[]{:S(2)}) copy-start(bf16[64,128,128]{2,1,0:T(8,128)(2,1)} %param.6) | copy-start | bytes 6291460
  10.9 15.1 %all-to-all-start = ((s32[32,2,3,128]{3,1,2,0:T(2,128)}), s32[32,2,3,128]{3,1,2,0:T(2,128)S(1)}, u32[]{:S(2)}, u32[]{:S(2)}) async-start(s32[32,2,3,128]{3,1,2,0:T(2,128)} %copy_select_fusion), calls=%async_computation | async-start | bytes 196608 | tf_op jit(solution)/shard_map/all_to_all | solution.py:214
  26.0 52.4 %all-to-all-start.1 = ((bf16[32,2,128,128]{3,2,1,0:T(8,128)(2,1)}), bf16[32,2,128,128]{3,2,1,0:T(8,128)(2,1)}, u32[]{:S(2)}, u32[]{:S(2)}) async-start(bf16[32,2,128,128]{3,2,1,0:T(8,128)(2,1)} %broadcast_select_fusion), calls=%async_computation.1 | async-start | bytes 4194304 | tf_op jit(solution)/shard_map/all_to_all | solution.py:214
  29.5 1.6 slice-start
  29.5 138.4 %all-gather.8.cloned.1.call-start = ((), (), s32[]{:S(2)}) async-start(), calls=%async_computation.3 | async-start | bytes 2162688 | tf_op jit(solution)/shard_map/all_gather | solution.py:256
  82.2 2.8 copy-start.2
  91.3 1.0 copy-start.8
  92.3 2.9 copy-start.7
  92.3 205.3 %all-gather.6.cloned.1.call-start = ((), (), s32[]{:S(2)}) async-start(), calls=%async_computation.2 | async-start | bytes 5242880 | tf_op jit(solution)/shard_map/all_gather | solution.py:269
  97.1 1.4 copy-start.9
  98.4 232.1 %all-gather.10.cloned.1.call-start = ((), (), s32[]{:S(2)}) async-start(), calls=%async_computation.4 | async-start | bytes 9437184 | tf_op jit(solution)/shard_map/all_gather | solution.py:266
  98.5 0.9 collective-permute-start
  99.4 1.0 copy-start.10
  176.9 1.9 copy-start.6
  278.0 2.0 copy-start.5
  304.0 2.8 copy-start.11
  368.1 14.7 %copy-start.3 = (bf16[64,128,128]{2,1,0:T(8,128)(2,1)S(1)}, bf16[64,128,128]{2,1,0:T(8,128)(2,1)}, u32[]{:S(2)}) copy-start(bf16[64,128,128]{2,1,0:T(8,128)(2,1)} %copy-done.2) | copy-start | bytes 6291460
  368.1 14.7 %copy-start.4 = (f32[2048,256]{1,0:T(8,128)S(1)}, f32[2048,256]{1,0:T(8,128)}, u32[]{:S(2)}) copy-start(f32[2048,256]{1,0:T(8,128)} %pad_maximum_fusion.panel_ref) | copy-start | bytes 6291460
  382.9 74.1 %copy-start.1 = (bf16[64,128,128]{2,1,0:T(8,128)(2,1)S(1)}, bf16[64,128,128]{2,1,0:T(8,128)(2,1)}, u32[]{:S(2)}) copy-start(bf16[64,128,128]{2,1,0:T(8,128)(2,1)} %param.6) | copy-start | bytes 6291460
Sparse Core Ops, SparseCore 0:
  92.4 75.4 all-gather.7
  169.5 33.4 all-gather.5
  205.2 125.3 all-gather.9

commit v2 on v1

--- a/solution.py
+++ b/solution.py
@@ -51,17 +51,30 @@
             t_ref[first + GROUP :, :] -= change[first + GROUP :, :]
 
 
-def factor_kernel(d_ref, m_ref, u_ref, t_ref, p_ref):
-    m_ref[...] = d_ref[...]
+def factor_kernel(row_devs, col_devs, d_ref, l_ref, inv_ref, m_ref, t_ref, p_ref):
     r = lax.broadcasted_iota(jnp.int32, (NB, NB), 0)
     c = lax.broadcasted_iota(jnp.int32, (NB, NB), 1)
+    for i in range(BLOCKS):
+        for j in range(i + 1):
+            source = (i * col_devs + j % col_devs) * NB
+            at = j // col_devs * NB
+            block = d_ref[source : source + NB, at : at + NB].astype(jnp.float32)
+            flipped = block.T
+            if i == j:
+                m_ref[i * NB : (i + 1) * NB, j * NB : (j + 1) * NB] = jnp.where(
+                    r >= c, block, flipped
+                )
+            else:
+                m_ref[i * NB : (i + 1) * NB, j * NB : (j + 1) * NB] = block
+                m_ref[j * NB : (j + 1) * NB, i * NB : (i + 1) * NB] = flipped
+    l_ref[...] = jnp.zeros_like(l_ref)
 
     def step(k, _):
         here = pl.ds(pl.multiple_of(k * NB, NB), NB)
         t_ref[:, :NB] = m_ref[here, here]
         t_ref[:, NB:] = jnp.where(r == c, 1.0, 0.0)
         factor_block(t_ref)
-        u_ref[here, :] = t_ref[:, :NB]
+        l_ref[here, here] = t_ref[:, :NB].T
         inverse = t_ref[:, NB:]
         p_ref[...] = jnp.dot(
             inverse, m_ref[here, :], precision=HIGHEST, preferred_element_type=jnp.float32
@@ -71,29 +84,37 @@
 
         def below(i, _):
             there = pl.ds(pl.multiple_of(i * NB, NB), NB)
+            part = p_ref[:, there]
+            l_ref[there, here] = part.T
             m_ref[there, here] = jnp.zeros((NB, NB), jnp.float32)
-            m_ref[there, :] -= dot_tn(p_ref[:, there], p_ref[...])
+            m_ref[there, :] -= dot_tn(part, p_ref[...])
             return 0
 
         lax.fori_loop(k + 1, BLOCKS, below, 0)
         return 0
 
     lax.fori_loop(0, BLOCKS, step, 0)
-
-
-def factor_diagonal(diag):
+    tall = lax.broadcasted_iota(jnp.int32, (WIDE, NB), 0)
+    lane = lax.broadcasted_iota(jnp.int32, (WIDE, NB), 1)
+    for j in range(BLOCKS):
+        at = j // col_devs * NB
+        inv_ref[j % col_devs, :, at : at + NB] = jnp.where(
+            tall >= lane + j * NB, m_ref[:, j * NB : (j + 1) * NB], 0.0
+        ).astype(jnp.bfloat16)
+
+
+def factor_diagonal(corner, row_devs, col_devs):
+    vmem = pl.BlockSpec(memory_space=pltpu.VMEM)
     return pl.pallas_call(
-        factor_kernel,
+        functools.partial(factor_kernel, row_devs, col_devs),
         out_shape=(
             jax.ShapeDtypeStruct((WIDE, WIDE), jnp.float32),
-            jax.ShapeDtypeStruct((WIDE, NB), jnp.float32),
-        ),
-        in_specs=[pl.BlockSpec(memory_space=pltpu.VMEM)],
-        out_specs=(
-            pl.BlockSpec(memory_space=pltpu.VMEM),
-            pl.BlockSpec(memory_space=pltpu.VMEM),
-        ),
+            jax.ShapeDtypeStruct((col_devs, WIDE, WIDE // col_devs), jnp.bfloat16),
+        ),
+        in_specs=[vmem],
+        out_specs=(vmem, vmem),
         scratch_shapes=[
+            pltpu.VMEM((WIDE, WIDE), jnp.float32),
             pltpu.VMEM((NB, 2 * NB), jnp.float32),
             pltpu.VMEM((NB, WIDE), jnp.float32),
         ],
@@ -101,11 +122,84 @@
         cost_estimate=pl.CostEstimate(
             flops=20 * WIDE**3, bytes_accessed=WIDE * WIDE * 8, transcendentals=WIDE
         ),
-    )(diag)
+    )(corner)
+
+
+def contract(a, b):
+    return lax.dot_general(a, b, (((1,), (1,)), ((), ())), preferred_element_type=jnp.float32)
+
+
+def solve_rows_kernel(*refs):
+    count = len(refs) - 4
+    raw = refs[:count]
+    inv_ref, own_ref, out_ref, panel_ref = refs[count:]
+    total = contract(raw[0][...], inv_ref[0])
+    panel = contract(raw[0][...], own_ref[0])
+    for d in range(1, count):
+        total += contract(raw[d][...], inv_ref[d])
+        panel += contract(raw[d][...], own_ref[d])
+    out_ref[...] = total.astype(jnp.bfloat16)
+    panel_ref[...] = panel
+
+
+def solve_rows(pieces, inverse, own_inverse):
+    rows, depth = pieces[0].shape
+    height = 512
+    vmem = pl.BlockSpec(memory_space=pltpu.VMEM)
+    return pl.pallas_call(
+        solve_rows_kernel,
+        out_shape=(
+            jax.ShapeDtypeStruct((rows, WIDE), jnp.bfloat16),
+            jax.ShapeDtypeStruct((rows, depth), jnp.float32),
+        ),
+        grid=(rows // height,),
+        in_specs=[pl.BlockSpec((height, depth), lambda g: (g, 0))] * len(pieces) + [vmem, vmem],
+        out_specs=(
+            pl.BlockSpec((height, WIDE), lambda g: (g, 0)),
+            pl.BlockSpec((height, depth), lambda g: (g, 0)),
+        ),
+        compiler_params=pltpu.CompilerParams(vmem_limit_bytes=32 * 1024 * 1024),
+        cost_estimate=pl.CostEstimate(
+            flops=2 * rows * WIDE * (WIDE + depth), bytes_accessed=rows * WIDE * 4, transcendentals=0
+        ),
+    )(*pieces, inverse, own_inverse)
+
+
+TALL = 4
+
+
+def solve_cols_kernel(raw_ref, inv_ref, out_ref):
+    count, depth = raw_ref.shape[0], raw_ref.shape[-1]
+    total = None
+    for q in range(count):
+        term = contract(raw_ref[q, 0].reshape(TALL * NB, depth), inv_ref[q])
+        total = term if total is None else total + term
+    out_ref[...] = total.astype(jnp.bfloat16).reshape(TALL, 1, NB, WIDE)
+
+
+def solve_cols(raw, inverse):
+    col_devs, ratio, lrb, _, depth = raw.shape
+    cols = ratio * lrb * NB
+    out = pl.pallas_call(
+        solve_cols_kernel,
+        out_shape=jax.ShapeDtypeStruct((lrb, ratio, NB, WIDE), jnp.bfloat16),
+        grid=(ratio, lrb // TALL),
+        in_specs=[
+            pl.BlockSpec((col_devs, 1, TALL, NB, depth), lambda o, g: (0, o, g, 0, 0)),
+            pl.BlockSpec(memory_space=pltpu.VMEM),
+        ],
+        out_specs=pl.BlockSpec((TALL, 1, NB, WIDE), lambda o, g: (g, o, 0, 0)),
+        compiler_params=pltpu.CompilerParams(vmem_limit_bytes=32 * 1024 * 1024),
+        cost_estimate=pl.CostEstimate(
+            flops=2 * cols * WIDE * WIDE, bytes_accessed=cols * WIDE * 4, transcendentals=0
+        ),
+    )(raw, inverse)
+    return out.reshape(cols, WIDE)
 
 
 STEP = 2
 CHUNK = 4
+STRIP = 8
 
 
 def update_kernel(
@@ -120,8 +214,16 @@
         return pl.ds(b * NB * nc + col, NB, stride=nc)
 
     last_row = (g * STEP + STEP - 1) * row_devs + row_here
+    linear = out_ref.reshape(STEP * NB, nc, NB)
     for chunk in range(0, nc, CHUNK):
         active = chunk * col_devs + col_here <= last_row
+        strip = chunk // STRIP * STRIP
+        strip_active = strip * col_devs + col_here <= last_row
+        if chunk == strip:
+
+            @pl.when(jnp.logical_not(strip_active))
+            def _(strip=strip):
+                linear[:, strip : strip + STRIP, :] = jnp.zeros((STEP * NB, STRIP, NB), jnp.float32)
 
         @pl.when(active)
         def _(chunk=chunk):
@@ -147,7 +249,7 @@
                         )
                         out_ref[place(b, col), :] = jnp.where(r + gap >= c, value, 0.0)
 
-        @pl.when(jnp.logical_not(active))
+        @pl.when(strip_active & jnp.logical_not(active))
         def _(chunk=chunk):
             for b in range(STEP):
                 for cc in range(CHUNK):
@@ -253,52 +355,46 @@
     added = added.reshape(lrb, own, NB, NB).transpose(0, 2, 1, 3).reshape(rows, own * NB)
     own_panel = (front_orig[0, :, 0, : own * NB] + added).astype(jnp.bfloat16)
 
-    corner = lax.all_gather(own_panel[:NB], ("frow", "fcol"), axis=0, tiled=False)
-    corner = corner.reshape(row_devs, col_devs, NB, own, NB)[:BLOCKS]
-    diag = corner.transpose(0, 2, 3, 1, 4).reshape(WIDE, WIDE).astype(jnp.float32)
-    diag = jnp.tril(diag) + jnp.tril(diag, -1).T
-
+    corner = lax.all_gather(own_panel[:NB], ("frow", "fcol"), axis=0, tiled=True)
+    corner = corner[: BLOCKS * col_devs * NB]
+
+    pieces = [own_panel]
+    for shift in range(1, col_devs):
+        route = [((q + shift) % col_devs, q) for q in range(col_devs)]
+        pieces.append(lax.ppermute(own_panel, "fcol", route))
     route = []
     for p in range(row_devs):
         for q in range(col_devs):
             route.append((p * col_devs + q, (q * ratio + p // col_devs) * col_devs + p % col_devs))
     turned = lax.ppermute(own_panel, ("frow", "fcol"), route)
     col_raw = lax.all_gather(turned, "frow", axis=0, tiled=False)
-    col_raw = col_raw.reshape(col_devs, ratio, lrb, NB, own, NB)
-    col_raw = col_raw.transpose(2, 1, 3, 4, 0, 5).reshape(cols, WIDE)
-    row_raw = lax.all_gather(own_panel, "fcol", axis=0, tiled=False)
-    row_raw = row_raw.reshape(col_devs, rows, own, NB).transpose(1, 2, 0, 3).reshape(rows, WIDE)
-
-    packed, diag_upper = factor_diagonal(diag)
-    inverse = jnp.tril(packed).astype(jnp.bfloat16)
-
-    def solve(raw, dtype):
-        return lax.dot_general(
-            raw, inverse, (((1,), (1,)), ((), ())), preferred_element_type=jnp.float32
-        ).astype(dtype)
-
-    rowf = solve(row_raw, jnp.bfloat16)
-    colf = solve(col_raw, jnp.bfloat16)
-    own_inverse = lax.dynamic_index_in_dim(
-        inverse.reshape(own, col_devs, NB, WIDE), col_here, axis=1, keepdims=False
-    ).reshape(own * NB, WIDE)
-    solved = lax.dot_general(
-        row_raw, own_inverse, (((1,), (1,)), ((), ())), preferred_element_type=jnp.float32
-    )
+    col_raw = col_raw.reshape(col_devs, ratio, lrb, NB, own * NB)
+
+    lower, inverse = factor_diagonal(corner, row_devs, col_devs)
+
+    turned_inverse = lax.dynamic_slice_in_dim(
+        jnp.concatenate([inverse, inverse], axis=0), col_here, col_devs, axis=0
+    )
+    own_inverse = jnp.concatenate(
+        [
+            lax.dynamic_slice_in_dim(turned_inverse, (col_here + j * col_devs) * NB, NB, axis=1)
+            for j in range(own)
+        ],
+        axis=1,
+    )
+    rowf, solved = solve_rows(pieces, turned_inverse, own_inverse)
     block = jnp.minimum(row_here, BLOCKS - 1)
-    above = lax.dynamic_slice(packed, (0, block * NB), (WIDE, NB))
-    on = lax.dynamic_slice(diag_upper, (block * NB, 0), (NB, NB)).T
-    corner_blocks = []
-    for j in range(own):
-        col_block = col_here + j * col_devs
-        left = lax.dynamic_slice(above, (col_block * NB, 0), (NB, NB)).T
-        corner_blocks.append(
-            jnp.where(col_block < block, left, jnp.where(col_block == block, on, 0.0))
-        )
-    corner_own = jnp.where(
-        row_here < BLOCKS, jnp.concatenate(corner_blocks, axis=1), solved[:NB]
-    )
-    panel = jnp.concatenate([corner_own, solved[NB:]], axis=0)
+    corner_own = jnp.concatenate(
+        [
+            lax.dynamic_slice(lower, (block * NB, (col_here + j * col_devs) * NB), (NB, NB))
+            for j in range(own)
+        ],
+        axis=1,
+    )
+    panel = jnp.concatenate(
+        [jnp.where(row_here < BLOCKS, corner_own, solved[:NB]), solved[NB:]], axis=0
+    )
+    colf = solve_cols(col_raw, inverse)
 
     out = update(
         front_orig.reshape(rows * nc, NB),

time: 471 us -> 377 us (0.80); the launches traced: 464 us -> 376 us
  local copies, waits for them, and re-layouts: 98.6 us -> 19.3 us
  starting transfers between devices: 11.8 us -> 42.7 us
  matrix products: 29 us -> 5.34 us
  other arithmetic: 23.6 us -> 7.71 us
  Pallas kernels: 160 us -> 168 us
  waiting for transfers between devices: 127 us -> 119 us
    reshape x4 -> x0, local copies, waits for them, and re-layouts: 33.7 us -> none  [the longest x1 14.2 us: shards(): col_raw = col_raw.transpose(2, 1, 3, 4, 0, 5).reshape(cols, WIDE)]
    ppermute x0 -> x3, starting transfers between devices: none -> 31.2 us  [shards(): pieces.append(lax.ppermute(own_panel, 'fcol', route))]
    all_gather x2 -> x1, waiting for transfers between devices: 67.4 us -> 41 us  [shards(): lax.all_gather(own_panel[:NB], ('frow', 'fcol'), axis=0, tiled=True)]
    dot_general x3 -> x0, matrix products: 22.3 us -> none  [the longest x2 21 us: solve(): lax.dot_general(raw, inverse, (((1,), (1,)), ((), ())), preferred_element...]
    pallas_call x1 -> x3, Pallas kernels: 85.8 us -> 105 us  [the longest x1 86.4 us: factor_diagonal(): pl.pallas_call(functools.partial(factor_kernel, row_devs, col_devs), out_...]
    all_gather x1, waiting for transfers between devices: 14.6 us -> 26.9 us  [shards(): col_raw = lax.all_gather(turned, 'frow', axis=0, tiled=False)]
    pallas_call x1, Pallas kernels: 74.1 us -> 63.3 us  [update(): pl.pallas_call(functools.partial(update_kernel, row_devs, col_devs, nc, o...]
    convert_element_type x3 -> x0, local copies, waits for them, and re-layouts: 10.3 us -> none  [the longest x2 8.98 us: shards(): corner.transpose(0, 2, 3, 1, 4).reshape(WIDE, WIDE).astype(jnp.float32)]
  transfers between devices with their start and end apart: 6 -> 8, of which waited for: 4 -> 4; matrix products, arithmetic and copies ran while one was open for 16% -> 2% of each run, Pallas kernels for 19% -> 25%
where the time goes in v2:
time: 377 us; the launch traced here: 376 us
  Pallas kernels  168 us (45%)
  waiting for transfers between devices  119 us (32%)
  starting transfers between devices  42.7 us (11%)
  local copies, waits for them, and re-layouts  19.3 us (5%)
  between operations  13.7 us (4%)
  other arithmetic  7.71 us (2%)
  matrix products  5.34 us (1%)
    pallas_call x1, Pallas kernels, factor_diagonal(): pl.pallas_call(functools.partial(factor_kernel, row_devs, col_devs), out_...  86.4 us
    pallas_call x1, Pallas kernels, update(): pl.pallas_call(functools.partial(update_kernel, row_devs, col_devs, nc, o...  63.3 us
    all_to_all x2, waiting for transfers between devices, exchange(): lax.all_to_all(x, ('frow', 'fcol'), split_axis=0, concat_axis=0, tiled=True)  51.2 us
    all_gather x1, waiting for transfers between devices, shards(): lax.all_gather(own_panel[:NB], ('frow', 'fcol'), axis=0, tiled=True)  41 us
    ppermute x3, starting transfers between devices, shards(): pieces.append(lax.ppermute(own_panel, 'fcol', route))  31.2 us
    all_gather x1, waiting for transfers between devices, shards(): col_raw = lax.all_gather(turned, 'frow', axis=0, tiled=False)  26.9 us
    unnamed x23, local copies, waits for them, and re-layouts  12.5 us
    pallas_call x1, Pallas kernels, solve_cols(): pl.pallas_call(solve_cols_kernel, out_shape=jax.ShapeDtypeStruct((lrb, ra...  11.3 us
  transfers between devices with their start and end apart: 8, of which 4 were waited for; matrix products, arithmetic and copies ran while one was open for 2% of the time, Pallas kernels for 25%

profile of v2, /device:TPU:0, one launch (start us, length us, event | category | flops | bytes accessed | tf_op | source)
XLA Modules:
  0.0 376.4 jit_solution(4254443218278369096)
XLA Ops:
  6.5 0.8 slice_bitcast_fusion.3
  7.6 0.7 multiply_add_fusion
  8.6 0.9 pad_add_fusion
  9.5 0.7 gather_fusion
  10.2 0.8 copy_select_fusion
  10.9 7.3 %all-to-all-start = ((s32[32,2,3,128]{3,1,2,0:T(2,128)}), s32[32,2,3,128]{3,1,2,0:T(2,128)S(1)}, u32[]{:S(2)}, u32[]{:S(2)}) async-start(s32[32,2,3,128]{3,1,2,0:T(2,128)} %copy_select_fusion), calls=%async_computation | async-start | bytes 196608 | tf_op jit(solution)/shard_map/all_to_all | solution.py:316
  18.2 2.1 gather_fusion.1
  20.4 3.2 broadcast_select_fusion
  23.5 2.5 all-to-all-done
  26.0 3.3 all-to-all-start.1
  29.6 48.7 %all-to-all-done.1 = bf16[32,2,128,128]{3,2,1,0:T(8,128)(2,1)S(1)} async-done(((bf16[32,2,128,128]{3,2,1,0:T(8,128)(2,1)}), bf16[32,2,128,128]{3,2,1,0:T(8,128)(2,1)S(1)}, u32[]{:S(2)}, u32[]{:S(2)}) %all-to-all-start.1) | async-done | bytes 2097184 | tf_op jit(solution)/shard_map/all_to_all | solution.py:316
  78.3 1.3 copy-done.9
  79.6 3.8 %fusion.9.tiles_ref = bf16[64,128,128]{2,1,0:T(8,128)(2,1)S(1)} fusion(s32[64,128]{1,0:T(8,128)S(1)} %get-tuple-element.18, bf16[64,128,128]{2,1,0:T(8,128)(2,1)} %bitcast.70, s32[64,128]{1,0:T(8,128)S(1)} %get-tuple-element.17), kind=kOutput, calls=%fused_computation.18 | convolution fusion | flops 541065216 | bytes 4259840 | tf_op jit(solution)/shard_map/axj,ayj->axy/dot_general | solution.py:310
  83.5 1.5 fusion.12
  85.0 1.6 copy.32
  86.6 0.3 fusion.2.refs_0_
  86.9 0.6 slice.49
  87.7 0.7 collective-permute-start.3
  88.4 1.0 copy-done.10
  89.5 15.9 %collective-permute-start.2 = (bf16[2048,256]{1,0:T(8,128)(2,1)S(1)}, bf16[2048,256]{1,0:T(8,128)(2,1)}, u32[]{:S(2)}, u32[]{:S(2)}) collective-permute-start(bf16[2048,256]{1,0:T(8,128)(2,1)S(1)} %fusion.2.refs_0_), channel_id=1, source_target_pairs={{3,0},{0,1},{1,2},{2,3},{7,4},{4,5},{5,6},{6,7},{11,8},{8,9},{9,10... | collective-permute-start | bytes 3145736 | tf_op jit(solution)/shard_map/ppermute | solution.py:364
  105.4 15.3 %collective-permute-start.1 = (bf16[2048,256]{1,0:T(8,128)(2,1)S(1)}, bf16[2048,256]{1,0:T(8,128)(2,1)}, u32[]{:S(2)}, u32[]{:S(2)}) collective-permute-start(bf16[2048,256]{1,0:T(8,128)(2,1)S(1)} %fusion.2.refs_0_), channel_id=1, source_target_pairs={{2,0},{3,1},{0,2},{1,3},{6,4},{7,5},{4,6},{5,7},{10,8},{11,9},{8,1... | collective-permute-start | bytes 3145736 | tf_op jit(solution)/shard_map/ppermute | solution.py:364
  120.8 41.0 %all-gather.4.cloned.1.call-done.d_ref = bf16[4096,256]{1,0:T(8,128)(2,1)} async-done(((bf16[128,256]{1,0:T(8,128)(2,1)}), bf16[4096,256]{1,0:T(8,128)(2,1)}) %all-gather.4.cloned.1.call-update) | async-done | bytes 2097168 | tf_op jit(solution)/shard_map/all_gather | solution.py:358
  161.8 1.6 copy-done.8
  163.3 86.4 %shard_map.55 = (f32[1024,1024]{1,0:T(8,128)S(1)}, bf16[4,1024,256]{2,1,0:T(8,128)(2,1)S(1)}) custom-call(bf16[4096,256]{1,0:T(8,128)(2,1)S(1)} %copy-done.8), custom_call_target="tpu_custom_call" | custom-call | flops 21474836480 | bytes 8388608 | tf_op jit(solution)/shard_map/pallas_call | solution.py:108
  250.4 7.4 %shard_map.56 = (bf16[2048,1024]{1,0:T(8,128)(2,1)S(1)}, f32[2048,256]{1,0:T(8,128)S(1)}) custom-call(bf16[2048,256]{1,0:T(8,128)(2,1)S(1)} %fusion.2.refs_0_, bf16[2048,256]{1,0:T(8,128)(2,1)} %collective-permute-done.refs_1_, bf16[2048,256]{1,0:T(8,128)(2,1)} %collective-permute-done.1.refs_2_, bf16[2048,256]{1,0:T(8,128)(2,1)} %collective-permute-done.2.refs_3_, ...), custom_call_target="tpu_custom_call" | custom-call | flops 5368709120 | bytes 8388608 | tf_op jit(solution)/shard_map/pallas_call | solution.py:149
  258.0 1.8 copy-done.6
  259.9 1.5 pad_maximum_fusion.panel_ref
  261.3 26.9 %all-gather.6.cloned.1.call-done = bf16[16384,256]{1,0:T(8,128)(2,1)} async-done(((bf16[2048,256]{1,0:T(8,128)(2,1)}), bf16[16384,256]{1,0:T(8,128)(2,1)}) %all-gather.6.cloned.1.call-update) | async-done | bytes 8388624 | tf_op jit(solution)/shard_map/all_gather | solution.py:370
  288.2 3.4 copy-done.7
  291.6 11.3 %shard_map.57 = bf16[16,2,128,1024]{3,2,1,0:T(8,128)(2,1)S(1)} custom-call(bf16[4,2,16,128,256]{4,3,2,1,0:T(8,128)(2,1)S(1)} %bitcast.66, bf16[4,1024,256]{2,1,0:T(8,128)(2,1)S(1)} %get-tuple-element.9.inv_ref), custom_call_target="tpu_custom_call" | custom-call | flops 8589934592 | bytes 16777216 | tf_op jit(solution)/shard_map/pallas_call | solution.py:183
  303.0 3.2 copy-done.5
  306.2 63.3 %shard_map.58 = f32[65536,128]{1,0:T(8,128)} custom-call(s32[64]{0:T(128)S(1)} %slice_reduce_fusion.ids, s32[2]{0:T(128)S(1)} %pad_add_fusion.1.pos, f32[65536,128]{1,0:T(8,128)} %bitcast.67, bf16[2048,1024]{1,0:T(8,128)(2,1)} %copy-done.6, bf16[4096,1024]{1,0:T(8,128)(2,1)} %bitcast.65, f32[2048,256]{1,0:T(8,128)S(1)} %copy-done.4, ...), custom_call_target="tpu_custom_call" | custom-call | flops 8589934592 | bytes 67108864 | tf_op jit(solution)/shard_map/pallas_call | solution.py:280
  (48 shorter events, 1.7 us)
Async XLA Ops:
  6.5 11.7 %copy-start = (bf16[64,128,128]{2,1,0:T(8,128)(2,1)S(1)}, bf16[64,128,128]{2,1,0:T(8,128)(2,1)}, u32[]{:S(2)}) copy-start(bf16[64,128,128]{2,1,0:T(8,128)(2,1)} %param.6) | copy-start | bytes 6291460
  10.9 15.1 %all-to-all-start = ((s32[32,2,3,128]{3,1,2,0:T(2,128)}), s32[32,2,3,128]{3,1,2,0:T(2,128)S(1)}, u32[]{:S(2)}, u32[]{:S(2)}) async-start(s32[32,2,3,128]{3,1,2,0:T(2,128)} %copy_select_fusion), calls=%async_computation | async-start | bytes 196608 | tf_op jit(solution)/shard_map/all_to_all | solution.py:316
  26.0 52.2 %all-to-all-start.1 = ((bf16[32,2,128,128]{3,2,1,0:T(8,128)(2,1)}), bf16[32,2,128,128]{3,2,1,0:T(8,128)(2,1)S(1)}, u32[]{:S(2)}, u32[]{:S(2)}) async-start(bf16[32,2,128,128]{3,2,1,0:T(8,128)(2,1)} %broadcast_select_fusion), calls=%async_computation.1 | async-start | bytes 4194304 | tf_op jit(solution)/shard_map/all_to_all | solution.py:316
  29.4 132.4 %all-gather.4.cloned.1.call-start = ((), (), s32[]{:S(2)}) async-start(), calls=%async_computation.2 | async-start | bytes 2162688 | tf_op jit(solution)/shard_map/all_gather | solution.py:358
  78.3 1.3 copy-start.9
  83.4 1.5 copy-start.2
  85.0 1.6 slice-start
  87.6 200.6 %all-gather.6.cloned.1.call-start = ((), (), s32[]{:S(2)}) async-start(), calls=%async_computation.3 | async-start | bytes 9437184 | tf_op jit(solution)/shard_map/all_gather | solution.py:370
  87.7 0.7 collective-permute-start.3
  88.4 1.0 copy-start.10
  89.5 160.9 %collective-permute-start.2 = (bf16[2048,256]{1,0:T(8,128)(2,1)S(1)}, bf16[2048,256]{1,0:T(8,128)(2,1)}, u32[]{:S(2)}, u32[]{:S(2)}) collective-permute-start(bf16[2048,256]{1,0:T(8,128)(2,1)S(1)} %fusion.2.refs_0_), channel_id=1, source_target_pairs={{3,0},{0,1},{1,2},{2,3},{7,4},{4,5},{5,6},{6,7},{11,8},{8,9},{9,10... | collective-permute-start | bytes 3145736 | tf_op jit(solution)/shard_map/ppermute | solution.py:364
  105.4 145.0 %collective-permute-start.1 = (bf16[2048,256]{1,0:T(8,128)(2,1)S(1)}, bf16[2048,256]{1,0:T(8,128)(2,1)}, u32[]{:S(2)}, u32[]{:S(2)}) collective-permute-start(bf16[2048,256]{1,0:T(8,128)(2,1)S(1)} %fusion.2.refs_0_), channel_id=1, source_target_pairs={{2,0},{3,1},{0,2},{1,3},{6,4},{7,5},{4,6},{5,7},{10,8},{11,9},{8,1... | collective-permute-start | bytes 3145736 | tf_op jit(solution)/shard_map/ppermute | solution.py:364
  120.7 129.7 %collective-permute-start = (bf16[2048,256]{1,0:T(8,128)(2,1)S(1)}, bf16[2048,256]{1,0:T(8,128)(2,1)}, u32[]{:S(2)}, u32[]{:S(2)}) collective-permute-start(bf16[2048,256]{1,0:T(8,128)(2,1)S(1)} %fusion.2.refs_0_), channel_id=1, source_target_pairs={{1,0},{2,1},{3,2},{0,3},{5,4},{6,5},{7,6},{4,7},{9,8},{10,9},{11,1... | collective-permute-start | bytes 3145736 | tf_op jit(solution)/shard_map/ppermute | solution.py:364
  161.8 1.6 copy-start.8
  257.9 2.0 copy-start.6
  288.2 3.4 copy-start.7
  291.6 14.6 %copy-start.3 = (bf16[64,128,128]{2,1,0:T(8,128)(2,1)S(1)}, bf16[64,128,128]{2,1,0:T(8,128)(2,1)}, u32[]{:S(2)}) copy-start(bf16[64,128,128]{2,1,0:T(8,128)(2,1)} %copy-done.2) | copy-start | bytes 6291460
  291.6 14.6 %copy-start.4 = (f32[2048,256]{1,0:T(8,128)S(1)}, f32[2048,256]{1,0:T(8,128)}, u32[]{:S(2)}) copy-start(f32[2048,256]{1,0:T(8,128)} %pad_maximum_fusion.panel_ref) | copy-start | bytes 6291460
  303.0 3.2 copy-start.5
  306.2 63.3 %copy-start.1 = (bf16[64,128,128]{2,1,0:T(8,128)(2,1)S(1)}, bf16[64,128,128]{2,1,0:T(8,128)(2,1)}, u32[]{:S(2)}) copy-start(bf16[64,128,128]{2,1,0:T(8,128)(2,1)} %param.6) | copy-start | bytes 6291460
Sparse Core Ops, SparseCore 0:
  87.7 73.9 all-gather.3
  163.9 124.3 all-gather.5
